TPU v7x, 768 devices: a whole 4x8x12 slice. The times are simulated.
768 devices in a mesh: group: 12 (over z), tensor: 64 (over x, y, core).
Axes of the slice: x: 4, y: 8, z: 12, core: 2. Of those that a mesh axis runs over, the one named last changes fastest.
Arguments:
- hidden: bfloat16 [12, 256, 14336], P('group', None, 'tensor'), may hold values from -6 to 6
- weights: bfloat16 [12, 14336, 4096], P('group', 'tensor'), may hold values from -0.125 to 0.125
- target: bfloat16 [12, 256, 4096], P('group', None, 'tensor'), may hold values from -6 to 6
- module: int32 [12, 1], replicated, may hold values from 0 to 3
- counts: int32 [12], replicated, may hold values from 1 to 256, 1664 in all
Outputs:
- update: bfloat16 [12, 14336, 4096], P('group', 'tensor')
Inputs may be any that keep to these rules, and one draw needn't show every extreme that they name: Every module number is used by at least one path.
All inputs are finite; a program needn't handle non-finite values.
Results may differ from a plain program's by a relative error of at most 0.0057.
Values may be sent and summed in bfloat16 or wider, within the bound.
A program may use at most 32 MiB of HBM per device.

v0:
```python
import math

import jax
import jax.numpy as jnp
from jax import lax
from jax.sharding import PartitionSpec as P


def average_paths(average_map, blocks):
    return jnp.einsum(
        "pq,qrc->prc", average_map, blocks.astype(jnp.float32), precision=lax.Precision.HIGHEST
    ).astype(jnp.bfloat16)


def on_device(hidden, weights, target, module, counts):
    activations = hidden[0]
    local_weights = weights[0]
    local_target = target[0]
    tokens_path = activations.shape[0]
    hidden_rows = local_weights.shape[0]
    factor = 1.0 / math.sqrt(tokens_path)
    groups = lax.axis_size("group")
    path_index = lax.axis_index("group")
    module_ids = module[:, 0]
    own_count = jnp.sum(jnp.where(jnp.arange(groups, dtype=jnp.int32) == path_index, counts, 0))
    outputs = lax.psum_scatter(
        lax.dot_general(
            local_weights, activations, (((0,), (1,)), ((), ())), preferred_element_type=jnp.float32
        ),
        "tensor",
        scatter_dimension=0,
        tiled=True,
    )
    live_mask = jnp.arange(tokens_path, dtype=jnp.int32) < own_count
    errors = jnp.where(
        live_mask[None, :], (outputs - local_target.T.astype(jnp.float32)) * factor, 0.0
    ).astype(jnp.bfloat16)
    delta = lax.dot_general(
        activations,
        lax.all_gather(errors, "tensor", axis=0, tiled=True),
        (((0,), (1,)), ((), ())),
        preferred_element_type=jnp.float32,
    ).astype(jnp.bfloat16)
    weight_float = counts.astype(jnp.float32)
    same_module = module_ids[:, None] == module_ids[None, :]
    numerator = jnp.where(same_module, weight_float[None, :], 0.0)
    average_map = numerator / jnp.sum(numerator, axis=1, keepdims=True)
    row_block = -(-hidden_rows // groups)
    padded = jnp.pad(delta, ((0, row_block * groups - hidden_rows), (0, 0)))[None]
    blocks = lax.all_to_all(padded, "group", split_axis=1, concat_axis=0, tiled=True)
    averaged = average_paths(average_map, blocks)
    returned = lax.all_to_all(averaged, "group", split_axis=0, concat_axis=1, tiled=True)
    update = returned[:, :hidden_rows, :]
    return update


def solution(mesh):
    in_specs = (
        P("group", None, "tensor"),
        P("group", "tensor", None),
        P("group", None, "tensor"),
        P(),
        P(),
    )
    out_specs = P("group", "tensor", None)
    return jax.shard_map(
        on_device, mesh=mesh, in_specs=in_specs, out_specs=out_specs, check_vma=False
    )
```

profile of v0, /device:TPU:1, one launch (start us, length us, event | category | flops | bytes accessed | tf_op | source)
XLA Modules:
  0.0 503.6 jit_solution(8277387810831171293)
XLA Ops:
  6.5 0.0 copy-start
  6.5 0.0 reduce-scatter.2.cloned.1.call-start
  6.5 1.5 copy-done
  8.0 3.6 fusion.2
  11.6 0.0 copy-start.4
  11.6 0.0 copy-start.2
  11.6 0.0 copy-start.1
  11.6 0.0 reduce-scatter.2.cloned.1.call-update
  11.7 0.0 all-gather.2.cloned.1.call-start
  11.7 0.6 copy-done.4
  12.3 0.6 fusion.19
  12.9 0.6 iota_compare_fusion
  13.6 161.8 %reduce-scatter.2.cloned.1.call-done = f32[64,256]{1,0:T(8,128)} async-done(((f32[4096,256]{1,0:T(8,128)}), f32[64,256]{1,0:T(8,128)}) %reduce-scatter.2.cloned.1.call-update) | async-done | bytes 65552 | tf_op jit(solution)/shard_map/reduce_scatter | solution.py:26
  175.4 0.0 copy-done.2
  175.4 1.5 fusion.9
  176.9 0.0 all-gather.2.cloned.1.call-update
  176.9 95.4 %all-gather.2.cloned.1.call-done = bf16[4096,256]{1,0:T(8,128)(2,1)} async-done(((bf16[64,256]{1,0:T(8,128)(2,1)}), bf16[4096,256]{1,0:T(8,128)(2,1)}) %all-gather.2.cloned.1.call-update) | async-done | bytes 2097168 | tf_op jit(solution)/shard_map/all_gather | solution.py:40
  272.2 0.0 copy-done.1
  272.3 2.4 fusion
  274.7 0.2 pad_bitcast_fusion
  274.8 6.1 %copy.18 = bf16[1,228,4096]{2,0,1:T(2,128)(2,1)} copy(bf16[1,228,4096]{2,1,0:T(8,128)(2,1)S(1)} %pad_bitcast_fusion) | data formatting | bytes 3735552 | tf_op jit(solution)/shard_map/broadcast_in_dim | solution.py:49
  280.9 0.5 broadcast.9
  281.4 13.5 %reduce.2 = bf16[228,4096]{1,0:T(8,128)(2,1)} reduce(bf16[228,1,4096]{2,1,0:T(2,128)(2,1)} %bitcast.35, bf16[]{:T(256)} %broadcast.9), dimensions={1}, to_apply=%bitcast.34.reduce_sub_computation | reduce | bytes 3735554
  295.0 5.5 %reshape.18 = bf16[12,2,38912]{2,1,0:T(2,128)(2,1)} reshape(bf16[228,4096]{1,0:T(8,128)(2,1)} %reduce.2) | data formatting | bytes 3735552
  300.5 0.0 copy-start.3
  300.5 10.1 %all-to-all-start = ((bf16[12,2,38912]{2,1,0:T(2,128)(2,1)}), bf16[12,2,38912]{2,1,0:T(2,128)(2,1)}, u32[]{:S(2)}, u32[]{:S(2)}) async-start(bf16[12,2,38912]{2,1,0:T(2,128)(2,1)} %reshape.18), calls=%async_computation.1 | async-start | bytes 3735552 | tf_op jit(solution)/shard_map/all_to_all | solution.py:50
  310.5 0.0 copy-done.3
  310.5 0.2 select_reduce_fusion
  310.7 64.7 %all-to-all-done = bf16[12,2,38912]{2,1,0:T(2,128)(2,1)} async-done(((bf16[12,2,38912]{2,1,0:T(2,128)(2,1)}), bf16[12,2,38912]{2,1,0:T(2,128)(2,1)}, u32[]{:S(2)}, u32[]{:S(2)}) %all-to-all-start) | async-done | bytes 1867808 | tf_op jit(solution)/shard_map/all_to_all | solution.py:50
  375.4 8.4 %reshape.19 = bf16[228,1,4096]{2,1,0:T(2,128)(2,1)} reshape(bf16[12,2,38912]{2,1,0:T(2,128)(2,1)} %all-to-all-done) | data formatting | bytes 3735552
  383.7 13.6 %bitcast_reduce_fusion = bf16[228,4096]{1,0:T(8,128)(2,1)} fusion(bf16[228,1,4096]{2,1,0:T(2,128)(2,1)} %reshape.19), kind=kLoop, calls=%fused_computation.27 | loop fusion | bytes 3735552 | tf_op jit(solution)/shard_map/all_to_all | solution.py:50
  397.3 3.1 all_to_all.9
  400.4 5.3 %convolution_convert_fusion = bf16[12,19,4096]{2,0,1:T(8,128)(2,1)S(1)} fusion(bf16[12,19,4096]{2,1,0:T(8,128)(2,1)} %all_to_all.9, f32[12]{0:T(128)S(1)} %select_reduce_fusion, f32[12]{0:T(128)S(1)} %get-tuple-element.5, s32[12]{0:T(128)S(1)} %bitcast.37), kind=kOutput, calls=%fused_computation | convolution fusion | flops 135414192 | bytes 3735696 | tf_op jit(solution)/shard_map/pq,qrc->prc/dot_general | solution.py:10
  405.7 1.1 copy.13
  406.8 83.9 %all_to_all.24 = bf16[12,19,4096]{2,1,0:T(8,128)(2,1)} all-to-all(bf16[12,19,4096]{2,1,0:T(8,128)(2,1)S(1)} %copy.13), channel_id=1, replica_groups=mesh['group'=12,'tensor'=64] {'group'}, dimensions={0} | all-to-all | bytes 3735552 | tf_op jit(solution)/shard_map/all_to_all | solution.py:52
  490.7 3.1 all_to_all.21
  493.8 2.9 slice.4
Async XLA Ops:
  6.5 1.5 copy-start
  6.5 168.9 %reduce-scatter.2.cloned.1.call-start = ((), (), s32[]{:S(2)}) async-start(), calls=%async_computation.3 | async-start | bytes 4259840 | tf_op jit(solution)/shard_map/reduce_scatter | solution.py:26
  11.6 0.7 copy-start.4
  11.6 163.8 %copy-start.2 = (bf16[1,256,64]{1,2,0:T(8,128)(2,1)S(1)}, bf16[1,256,64]{1,2,0:T(8,128)(2,1)}, u32[]{:S(2)}) copy-start(bf16[1,256,64]{1,2,0:T(8,128)(2,1)} %param.7) | copy-start | bytes 98308
  11.6 260.6 %copy-start.1 = (bf16[1,256,224]{1,2,0:T(8,128)(2,1)S(1)}, bf16[1,256,224]{1,2,0:T(8,128)(2,1)}, u32[]{:S(2)}) copy-start(bf16[1,256,224]{1,2,0:T(8,128)(2,1)} %param.5) | copy-start | bytes 344068
  11.7 260.6 %all-gather.2.cloned.1.call-start = ((), (), s32[]{:S(2)}) async-start(), calls=%async_computation.4 | async-start | bytes 2129920 | tf_op jit(solution)/shard_map/all_gather | solution.py:40
  300.5 10.1 %copy-start.3 = (s32[12,1]{0,1:T(1,128)S(1)}, s32[12,1]{0,1:T(1,128)}, u32[]{:S(2)}) copy-start(s32[12,1]{0,1:T(1,128)} %param.8) | copy-start | bytes 148
  300.5 74.9 %all-to-all-start = ((bf16[12,2,38912]{2,1,0:T(2,128)(2,1)}), bf16[12,2,38912]{2,1,0:T(2,128)(2,1)}, u32[]{:S(2)}, u32[]{:S(2)}) async-start(bf16[12,2,38912]{2,1,0:T(2,128)(2,1)} %reshape.18), calls=%async_computation.1 | async-start | bytes 3735552 | tf_op jit(solution)/shard_map/all_to_all | solution.py:50
Sparse Core Ops, SparseCore 0:
  12.6 162.6 reduce-scatter.1
  180.0 92.1 all-gather.1
where the time goes:
time: 508 us; the launch traced here: 504 us
  waiting for transfers between devices  322 us (63%)
  blocking collectives  83.9 us (17%)
  local copies, waits for them, and re-layouts  46.5 us (9%)
  other arithmetic  16.5 us (3%)
  between operations  13.5 us (3%)
  matrix products  11.3 us (2%)
  starting transfers between devices  10.1 us (2%)
    reduce_scatter x1, waiting for transfers between devices, on_device(): lax.psum_scatter(lax.dot_general(local_weights, activations, (((0,), (1,)...  162 us
    all_gather x1, waiting for transfers between devices, on_device(): lax.all_gather(errors, 'tensor', axis=0, tiled=True)  95.4 us
    all_to_all x1, blocking collectives, on_device(): lax.all_to_all(averaged, 'group', split_axis=0, concat_axis=1, tiled=True)  83.9 us
    all_to_all x1, waiting for transfers between devices, on_device(): lax.all_to_all(padded, 'group', split_axis=1, concat_axis=0, tiled=True)  64.7 us
    all_to_all x2, local copies, waits for them, and re-layouts, on_device(): lax.all_to_all(padded, 'group', split_axis=1, concat_axis=0, tiled=True)  16.7 us
    unnamed x13, local copies, waits for them, and re-layouts  16.4 us
    unnamed x1, other arithmetic  13.5 us
  transfers between devices with their start and end apart: 3, of which 3 were waited for; matrix products, arithmetic and copies ran while one was open for 0% of the time, Pallas kernels for 0%

commit v1 on v0

v1 whole, which is shorter than its diff:
```python
import functools
import math

import jax
import jax.numpy as jnp
from jax import lax
from jax.experimental import pallas as pl
from jax.experimental.pallas import tpu as pltpu
from jax.sharding import PartitionSpec as P

MESH = pl.DeviceIdType.MESH
BF = jnp.bfloat16
F32 = jnp.float32
LANES = 128


def kernel(X, Y, Z, RC, h_ref, w_ref, t_ref, m_ref, n_ref, o_ref,
           hp, tp, tr, hz, own, sibs, sibr, xs, xr, ys, yr, ez, sel, hc, ea,
           t_sem, h_send, h_recv, sib_send, sib_recv, x_send, x_recv, y_send, y_recv, e_send, e_recv, a_send, a_recv, a_sib):
    z = lax.axis_index("group")
    t = lax.axis_index("tensor")
    x, y, c = t // (2 * Y), (t // 2) % Y, t % 2
    tokens, rows = h_ref.shape
    half = tokens // 2
    other = 1 - c

    def wrap(value, size):
        return lax.rem(value + 2 * size, size)

    def at(px, py, pz, pc):
        return (pz, (px * Y + py) * 2 + pc)

    def copy(src, dst, send, recv, device):
        return pltpu.make_async_remote_copy(
            src_ref=src, dst_ref=dst, send_sem=send, recv_sem=recv, device_id=device, device_id_type=MESH
        )

    sibling = at(x, y, z, other)

    barrier = pltpu.get_barrier_semaphore()

    def greet(device):
        pl.semaphore_signal(barrier, inc=1, device_id=device, device_id_type=MESH)

    greet(sibling)
    for d in range(1, X):
        greet(at(wrap(x + d, X), y, z, c))
    for d in range(1, Y):
        greet(at(x, wrap(y + d, Y), z, c))
    for d in range(1, Z):
        greet(at(x, y, wrap(z + d, Z), c))

    slot = lax.broadcasted_iota(jnp.int32, (tokens, tokens), 0)
    token = lax.broadcasted_iota(jnp.int32, (tokens, tokens), 1)
    order = jnp.where(token == 2 * slot - jnp.where(slot >= half, tokens - 1, 0), 1.0, 0.0).astype(BF)
    hperm = jnp.dot(order, h_ref[...], preferred_element_type=F32)
    tperm = jnp.dot(order, t_ref[...], preferred_element_type=F32).astype(BF)
    twice = jnp.concatenate([tperm, tperm], axis=1)
    hturn = hperm.T.astype(BF)
    for k in range(2):
        hp[k] = hperm[k * half:(k + 1) * half].astype(BF)
        tp[k] = twice[k * half:(k + 1) * half]
        hz[z, k] = hturn[:, k * half:(k + 1) * half]

    pl.semaphore_wait(barrier, 1 + (X - 1) + (Y - 1) + (Z - 1))

    up, down = at(x, y, wrap(z + 1, Z), c), at(x, y, wrap(z - 1, Z), c)
    up_hops, down_hops = Z // 2, Z - 1 - Z // 2

    def hidden_copy(way, hop, k):
        source = wrap(z - (hop - 1), Z) if way == 0 else wrap(z + (hop - 1), Z)
        return copy(hz.at[source, k], hz.at[source, k], h_send.at[way, hop - 1, k], h_recv.at[source, k],
                    up if way == 0 else down)

    def hidden_arrived(way, hop, k):
        source = wrap(z - hop, Z) if way == 0 else wrap(z + hop, Z)
        copy(hz.at[source, k], hz.at[source, k], h_send.at[way, hop - 1, k], h_recv.at[source, k], up).wait_recv()

    def hidden_hop(hop):
        for k in range(2):
            for way, hops in ((0, up_hops), (1, down_hops)):
                if 1 < hop <= hops + 1:
                    hidden_arrived(way, hop - 1, k)
                if hop <= hops:
                    hidden_copy(way, hop, k).start()

    hidden_hop(1)
    target_copy = copy(tp.at[other], tr, t_sem.at[0], t_sem.at[1], sibling)
    target_copy.start()

    def sib_copy(k):
        return copy(sibs.at[k], sibr.at[k], sib_send.at[k], sib_recv.at[k], sibling)

    def partial_step(k, carry):
        to_y = wrap(y + 1 + k, Y)
        columns = jnp.concatenate(
            [w_ref[:, pl.ds(pl.multiple_of((i * Y + to_y) * LANES, LANES), LANES)] for i in range(X)], axis=1
        )
        theirs = jnp.dot(hp[other], columns, preferred_element_type=F32).astype(BF)
        for i in range(X):
            sibs[k, i] = theirs[:, i * LANES:(i + 1) * LANES]
        sib_copy(k).start()
        mine = jnp.dot(hp[c], columns, preferred_element_type=F32)
        for i in range(X):
            own[k, i] = mine[:, i * LANES:(i + 1) * LANES]
        return carry

    lax.fori_loop(0, Y, partial_step, 0)
    hidden_hop(2)

    def x_copy(k, d):
        return copy(xs.at[k, wrap(x + d, X)], xr.at[k, d - 1], x_send.at[k, d - 1], x_recv.at[k, d - 1],
                    at(wrap(x + d, X), y, z, c))

    def x_step(k, carry):
        sib_copy(k).wait_recv()
        for i in range(X):
            value = own[k, i] + sibr[k, i].astype(F32)
            own[k, i] = value
            xs[k, i] = value.astype(BF)
        for d in range(1, X):
            x_copy(k, d).start()
        return carry

    lax.fori_loop(0, Y, x_step, 0)
    hidden_hop(3)

    def y_copy(k):
        return copy(ys.at[k], yr.at[k], y_send.at[k], y_recv.at[k], at(x, wrap(y + 1 + k, Y), z, c))

    def x_sum(k):
        value = own[k, x]
        for d in range(1, X):
            x_copy(k, d).wait_recv()
            value = value + xr[k, d - 1].astype(F32)
        return value

    def y_step(k, carry):
        ys[k] = x_sum(k).astype(BF)
        y_copy(k).start()
        return carry

    stop = (Y - 1) // 3
    lax.fori_loop(0, stop, y_step, 0)
    hidden_hop(4)
    lax.fori_loop(stop, 2 * stop, y_step, 0)
    hidden_hop(5)
    lax.fori_loop(2 * stop, Y - 1, y_step, 0)
    hidden_hop(6)
    total = x_sum(Y - 1)

    def y_sum(k, value):
        y_copy(k).wait_recv()
        return value + yr[k].astype(F32)

    total = lax.fori_loop(0, Y - 1, y_sum, total)

    my_module = m_ref[z]
    weight_sum = jnp.int32(0)
    live = []
    start = [jnp.int32(0), jnp.int32(0)]
    for q in range(Z):
        same = jnp.where(m_ref[q] == my_module, 1, 0)
        weight_sum = weight_sum + same * n_ref[q]
        entry = []
        for k in range(2):
            number = same * lax.div(n_ref[q] + 1 - k, 2)
            entry.append((start[k], number))
            start[k] = start[k] + number
        live.append(entry)
    share = jnp.full((1, LANES), n_ref[z], jnp.int32).astype(F32) / jnp.full((1, LANES), weight_sum, jnp.int32).astype(F32)

    target_copy.wait_recv()
    low = jnp.where(c == 0, tp[c].astype(F32), tr[...].astype(F32))
    high = jnp.where(c == 0, tr[...].astype(F32), tp[c].astype(F32))
    lane = lax.broadcasted_iota(jnp.int32, (half, LANES), 1)
    target = jnp.where(lane < LANES // 2, low, high)
    ez[z] = ((total - target) * (1.0 / math.sqrt(tokens)) * share).astype(BF)

    def e_copy(d):
        return copy(ez.at[z], ez.at[z], e_send.at[d - 1], e_recv.at[z], at(x, y, wrap(z + d, Z), c))

    for d in [k // 2 + 1 if k % 2 == 0 else Z - 1 - k // 2 for k in range(Z - 1)]:
        e_copy(d).start()

    gap = lax.broadcasted_iota(jnp.int32, (RC, half), 0) - lax.broadcasted_iota(jnp.int32, (RC, half), 1)
    column = lax.broadcasted_iota(jnp.int32, (RC, half), 1)
    for k in range(2):
        for q in range(Z):
            first, number = live[q][k]
            sel[k, :, q * half:(q + 1) * half] = jnp.where((gap == first) & (column < number), 1.0, 0.0).astype(BF)

    def e_arrived(d):
        source = wrap(z + d, Z)
        copy(ez.at[source], ez.at[source], e_send.at[0], e_recv.at[source], up).wait_recv()

    for d in range(1, Z):
        e_arrived(d)
    errors = ez[...].reshape(Z * half, LANES)
    ea[x * Y + y, c] = jnp.dot(sel[c], errors, preferred_element_type=F32).astype(BF)

    def block(px, py):
        return wrap(px, X) * Y + wrap(py, Y)

    def a_copy(j, kind):
        if kind == 0:
            device = at(x, wrap(y + 1, Y), z, c)
        elif kind == 1:
            device = at(x, wrap(y - 1, Y), z, c)
        elif kind == 2:
            return copy(ea.at[j, c], ea.at[j, c], a_send.at[j, 2], a_sib.at[j], sibling)
        else:
            device = at(wrap(x + kind - 2, X), y, z, c)
        return copy(ea.at[j, c], ea.at[j, c], a_send.at[j, kind], a_recv.at[j], device)

    y_up, y_down = Y // 2, Y - 1 - Y // 2
    x_kinds = tuple(range(3, 2 + X))

    def spread(phase):
        def visit(j, kinds, arrives=True):
            if phase == 0 and arrives:
                a_copy(j, 0).wait_recv()
            for kind in kinds:
                if phase == 0:
                    a_copy(j, kind).start()
                else:
                    a_copy(j, kind).wait_send()

        visit(block(x, y), (0, 1, 2) + x_kinds, arrives=False)

        @pl.when(c == 0)
        def _():
            for d in range(1, X):
                visit(block(x - d, y), (0, 1, 2))

            def hop_step(i, carry):
                hop, px = i // X + 1, x - i % X
                j = block(px, y - hop)

                @pl.when(hop < y_up)
                def _():
                    visit(j, (0, 2))

                @pl.when(hop == y_up)
                def _():
                    visit(j, (2,))

                j2 = block(px, y + hop)

                @pl.when(hop < y_down)
                def _():
                    visit(j2, (1, 2))

                @pl.when(hop == y_down)
                def _():
                    visit(j2, (2,))

                return carry

            lax.fori_loop(0, X * y_up, hop_step, 0)

        @pl.when(c == 1)
        def _():
            for hop in range(1, y_up + 1):
                visit(block(x, y - hop), ((0,) if hop < y_up else ()) + x_kinds + (2,))
                if hop <= y_down:
                    visit(block(x, y + hop), ((1,) if hop < y_down else ()) + x_kinds + (2,))

            def side_step(i, carry):
                hop, d = i // (X - 1), i % (X - 1) + 1
                visit(block(x - d, y - hop), (2,))

                @pl.when((hop > 0) & (hop <= y_down))
                def _():
                    visit(block(x - d, y + hop), (2,))

                return carry

            lax.fori_loop(0, (y_up + 1) * (X - 1), side_step, 0)

    hidden_hop(7)
    for k in range(2):
        wide = jnp.concatenate([hz[q, k] for q in range(Z)], axis=1)
        hc[k] = lax.dot_general(wide, sel[k], (((1,), (1,)), ((), ())), preferred_element_type=F32).astype(BF)

    spread(0)

    def out_step(i, carry):
        for n in range(2):
            copy(ea.at[2 * i + n, other], ea.at[2 * i + n, other], a_send.at[2 * i + n, 2], a_sib.at[2 * i + n], sibling).wait_recv()
        value = None
        for k in range(2):
            right = jnp.concatenate([ea[2 * i, k], ea[2 * i + 1, k]], axis=1)
            term = jnp.dot(hc[k], right, preferred_element_type=F32)
            value = term if value is None else value + term
        o_ref[:, pl.ds(pl.multiple_of(i * 2 * LANES, 2 * LANES), 2 * LANES)] = value.astype(BF)
        return carry

    lax.fori_loop(0, X * Y // 2, out_step, 0)

    target_copy.wait_send()
    for k in range(2):
        for way, hops in ((0, up_hops), (1, down_hops)):
            for hop in range(1, hops + 1):
                hidden_copy(way, hop, k).wait_send()

    def sent_step(k, carry):
        sib_copy(k).wait_send()
        for d in range(1, X):
            x_copy(k, d).wait_send()
        return carry

    lax.fori_loop(0, Y, sent_step, 0)

    def sent_y(k, carry):
        y_copy(k).wait_send()
        return carry

    lax.fori_loop(0, Y - 1, sent_y, 0)
    for d in range(1, Z):
        e_copy(d).wait_send()
    spread(1)


def call(X, Y, Z, RC, hidden, weights, target, module, counts):
    tokens, rows = hidden.shape
    features = weights.shape[1]
    half = tokens // 2
    vmem = pl.BlockSpec(memory_space=pltpu.VMEM)
    smem = pl.BlockSpec(memory_space=pltpu.SMEM)
    dma = pltpu.SemaphoreType.DMA
    return pl.pallas_call(
        functools.partial(kernel, X, Y, Z, RC),
        out_shape=jax.ShapeDtypeStruct((rows, features), BF),
        in_specs=[vmem, vmem, vmem, smem, smem],
        out_specs=vmem,
        scratch_shapes=[
            pltpu.VMEM((2, half, rows), BF),
            pltpu.VMEM((2, half, LANES), BF),
            pltpu.VMEM((half, LANES), BF),
            pltpu.VMEM((Z, 2, rows, half), BF),
            pltpu.VMEM((Y, X, half, LANES), F32),
            pltpu.VMEM((Y, X, half, LANES), BF),
            pltpu.VMEM((Y, X, half, LANES), BF),
            pltpu.VMEM((Y, X, half, LANES), BF),
            pltpu.VMEM((Y, X - 1, half, LANES), BF),
            pltpu.VMEM((Y - 1, half, LANES), BF),
            pltpu.VMEM((Y - 1, half, LANES), BF),
            pltpu.VMEM((Z, half, LANES), BF),
            pltpu.VMEM((2, RC, Z * half), BF),
            pltpu.VMEM((2, rows, RC), BF),
            pltpu.VMEM((X * Y, 2, RC, LANES), BF),
            dma((2,)),
            dma((2, Z // 2, 2)),
            dma((Z, 2)),
            dma((Y,)),
            dma((Y,)),
            dma((Y, X - 1)),
            dma((Y, X - 1)),
            dma((Y - 1,)),
            dma((Y - 1,)),
            dma((Z - 1,)),
            dma((Z,)),
            dma((X * Y, 2 + X)),
            dma((X * Y,)),
            dma((X * Y,)),
        ],
        compiler_params=pltpu.CompilerParams(collective_id=0, has_side_effects=True, vmem_limit_bytes=56 * 2**20),
        name="step",
    )(hidden, weights, target, module, counts)


def on_device(X, Y, Z, RC, hidden, weights, target, module, counts):
    return call(X, Y, Z, RC, hidden[0], weights[0], target[0], module[:, 0], counts)[None]


def solution(mesh):
    in_specs = (
        P("group", None, "tensor"),
        P("group", "tensor", None),
        P("group", None, "tensor"),
        P(),
        P(),
    )
    return jax.shard_map(
        functools.partial(on_device, 4, 8, 12, 896),
        mesh=mesh, in_specs=in_specs, out_specs=P("group", "tensor", None), check_vma=False,
    )
```

time: 508 us -> 132 us (0.26)
  waiting for transfers between devices: 322 us -> 0 us
  Pallas kernels: 0 us -> 126 us
  blocking collectives: 83.9 us -> 0 us
  local copies, waits for them, and re-layouts: 46.5 us -> 6.06 us
  other arithmetic: 16.5 us -> 0 us
  between operations: 13.5 us -> 0.01 us
  matrix products: 11.3 us -> 0 us
  starting transfers between devices: 10.1 us -> 0 us
    reduce_scatter x1 -> x0, waiting for transfers between devices: 162 us -> none  [on_device(): lax.psum_scatter(lax.dot_general(local_weights, activations, (((0,), (1,)...]
    pallas_call x0 -> x1, Pallas kernels: none -> 126 us  [call(): pl.pallas_call(functools.partial(kernel, X, Y, Z, RC), out_shape=jax.Shap...]
    all_gather x1 -> x0, waiting for transfers between devices: 95.4 us -> none  [on_device(): lax.all_gather(errors, 'tensor', axis=0, tiled=True)]
    all_to_all x1 -> x0, blocking collectives: 83.9 us -> none  [on_device(): lax.all_to_all(averaged, 'group', split_axis=0, concat_axis=1, tiled=True)]
    all_to_all x1 -> x0, waiting for transfers between devices: 64.7 us -> none  [on_device(): lax.all_to_all(padded, 'group', split_axis=1, concat_axis=0, tiled=True)]
    all_to_all x3 -> x0, local copies, waits for them, and re-layouts: 19.8 us -> none  [the longest x2 16.7 us: on_device(): lax.all_to_all(padded, 'group', split_axis=1, concat_axis=0, tiled=True)]
    unnamed x1 -> x0, other arithmetic: 13.5 us -> none
    dot_general x3 -> x0, matrix products: 11.3 us -> none  [the longest x1 5.27 us: average_paths(): jnp.einsum('pq,qrc->prc', average_map, blocks.astype(jnp.float32), precis...]
  transfers between devices with their start and end apart: 3 -> 0, of which waited for: 3 -> 0; matrix products, arithmetic and copies ran while one was open for 0% -> 0% of each run, Pallas kernels for 0% -> 0%
where the time goes in v1:
time: 132 us
  Pallas kernels  126 us (95%)
  local copies, waits for them, and re-layouts  6.06 us (5%)
    pallas_call x1, Pallas kernels, call(): pl.pallas_call(functools.partial(kernel, X, Y, Z, RC), out_shape=jax.Shap...  126 us
    unnamed x3, local copies, waits for them, and re-layouts  6.06 us

profile of v1, /device:TPU:1, one launch (start us, length us, event | category | flops | bytes accessed | tf_op | source)
XLA Modules:
  0.0 131.8 jit_solution(5621786550379352653)
XLA Ops:
  0.0 1.5 %copy.7 = bf16[1,256,64]{2,1,0:T(8,128)(2,1)} copy(bf16[1,256,64]{1,2,0:T(8,128)(2,1)} %param.7) | data formatting | bytes 65536 | tf_op args[2]
  1.5 1.7 %copy.6 = bf16[1,256,224]{2,1,0:T(8,128)(2,1)} copy(bf16[1,256,224]{1,2,0:T(8,128)(2,1)} %param.5) | data formatting | bytes 229376 | tf_op args[0]
  3.1 125.7 %step.1 = bf16[224,4096]{1,0:T(8,128)(2,1)} custom-call(bf16[256,224]{1,0:T(8,128)(2,1)} %bitcast.7, bf16[224,4096]{1,0:T(8,128)(2,1)} %bitcast.6, bf16[256,64]{1,0:T(8,128)(2,1)} %bitcast.8, s32[12]{0:T(128)} %bitcast.9, s32[12]{0:T(128)} %n_ref.1), custom_call_target="tpu_custom_call" | custom-call | tf_op jit(solution)/shard_map/step/pallas_call | solution.py:332
  128.9 2.9 %copy.9 = bf16[1,224,4096]{2,1,0:T(8,128)(2,1)} copy(bf16[1,224,4096]{2,1,0:T(8,128)(2,1)} %bitcast.5) | data formatting | bytes 3670016

commit v2 on v1

v2 whole, which is shorter than its diff:
```python
import functools
import math

import jax
import jax.numpy as jnp
from jax import lax
from jax.experimental import pallas as pl
from jax.experimental.pallas import tpu as pltpu
from jax.sharding import PartitionSpec as P

MESH = pl.DeviceIdType.MESH
BF = jnp.bfloat16
F32 = jnp.float32
LANES = 128
SIZES = (160, 192, 224, 448)


def kernel(X, Y, Z, RC, h_hbm, w_hbm, t_hbm, m_ref, n_ref, o_ref,
           h_ref, w_ref, t_ref, hp, tp, tr, hz, own, sibs, sibr, xs, xr, ys, yr, ez, pick, sel, hc, ea,
           load, t_sem, h_send, h_recv, sib_send, sib_recv, x_send, x_recv, y_send, y_recv, e_send, e_recv, a_send, a_recv, a_sib):
    z = lax.axis_index("group")
    t = lax.axis_index("tensor")
    x, y, c = t // (2 * Y), (t // 2) % Y, t % 2
    rows, tokens = h_ref.shape
    half = tokens // 2
    part = half // 2
    other = 1 - c

    def wrap(value, size):
        return lax.rem(value + 2 * size, size)

    def at(px, py, pz, pc):
        return (pz, (px * Y + py) * 2 + pc)

    def copy(src, dst, send, recv, device):
        return pltpu.make_async_remote_copy(
            src_ref=src, dst_ref=dst, send_sem=send, recv_sem=recv, device_id=device, device_id_type=MESH
        )

    sibling = at(x, y, z, other)
    loads = [
        pltpu.make_async_copy(source, target, load.at[i])
        for i, (source, target) in enumerate(((h_hbm, h_ref), (t_hbm, t_ref), (w_hbm, w_ref)))
    ]
    for item in loads:
        item.start()

    barrier = pltpu.get_barrier_semaphore()

    def greet(device):
        pl.semaphore_signal(barrier, inc=1, device_id=device, device_id_type=MESH)

    greet(sibling)
    for d in range(1, X):
        greet(at(wrap(x + d, X), y, z, c))
    for d in range(1, Y):
        greet(at(x, wrap(y + d, Y), z, c))
    for d in range(1, Z):
        greet(at(x, y, wrap(z + d, Z), c))

    slot = lax.broadcasted_iota(jnp.int32, (tokens, tokens), 0)
    token = lax.broadcasted_iota(jnp.int32, (tokens, tokens), 1)
    quarter = slot // part
    order = jnp.where(token == 4 * (slot % part) + 2 * (quarter % 2) + quarter // 2, 1.0, 0.0).astype(BF)
    loads[0].wait()
    loads[1].wait()
    by_last = (((1,), (1,)), ((), ()))
    hperm = lax.dot_general(order, h_ref[...], by_last, preferred_element_type=F32)
    hturn = lax.dot_general(h_ref[...], order, by_last, preferred_element_type=F32)
    tperm = lax.dot_general(order, t_ref[...], by_last, preferred_element_type=F32).astype(BF)
    twice = jnp.concatenate([tperm, tperm], axis=1)
    for k in range(2):
        hp[k] = hperm[k * half:(k + 1) * half].astype(BF)
        tp[k] = twice[k * half:(k + 1) * half]
        hz[z, k] = hturn[:, k * half:(k + 1) * half].astype(BF)

    pl.semaphore_wait(barrier, 1 + (X - 1) + (Y - 1) + (Z - 1))

    up, down = at(x, y, wrap(z + 1, Z), c), at(x, y, wrap(z - 1, Z), c)
    up_hops, down_hops = Z // 2, Z - 1 - Z // 2

    def hidden_copy(way, hop, k):
        source = wrap(z - (hop - 1), Z) if way == 0 else wrap(z + (hop - 1), Z)
        return copy(hz.at[source, k], hz.at[source, k], h_send.at[way, hop - 1, k], h_recv.at[source, k],
                    up if way == 0 else down)

    def hidden_arrived(way, hop, k):
        source = wrap(z - hop, Z) if way == 0 else wrap(z + hop, Z)
        copy(hz.at[source, k], hz.at[source, k], h_send.at[way, hop - 1, k], h_recv.at[source, k], up).wait_recv()

    def hidden_hop(hop):
        for k in range(2):
            for way, hops in ((0, up_hops), (1, down_hops)):
                if 1 < hop <= hops + 1:
                    hidden_arrived(way, hop - 1, k)
                if hop <= hops:
                    hidden_copy(way, hop, k).start()

    hidden_hop(1)
    target_copy = copy(tp.at[other], tr, t_sem.at[0], t_sem.at[1], sibling)
    target_copy.start()

    def sib_copy(k):
        return copy(sibs.at[k], sibr.at[k], sib_send.at[k], sib_recv.at[k], sibling)

    def partial_step(k, carry):
        to_y = wrap(y + 1 + k, Y)
        columns = jnp.concatenate(
            [w_ref[:, pl.ds(pl.multiple_of((i * Y + to_y) * LANES, LANES), LANES)] for i in range(X)], axis=1
        )
        theirs = jnp.dot(hp[other], columns, preferred_element_type=F32).astype(BF)
        for i in range(X):
            sibs[k, i] = theirs[:, i * LANES:(i + 1) * LANES]
        sib_copy(k).start()
        mine = jnp.dot(hp[c], columns, preferred_element_type=F32)
        for i in range(X):
            own[k, i] = mine[:, i * LANES:(i + 1) * LANES]
        return carry

    loads[2].wait()
    lax.fori_loop(0, Y, partial_step, 0)

    def x_copy(p, k, d):
        return copy(xs.at[p, k, wrap(x + d, X)], xr.at[p, k, d - 1], x_send.at[p, k, d - 1], x_recv.at[p, k, d - 1],
                    at(wrap(x + d, X), y, z, c))

    def x_step(k, carry):
        sib_copy(k).wait_recv()
        for i in range(X):
            value = own[k, i] + sibr[k, i].astype(F32)
            own[k, i] = value
            for p in range(2):
                xs[p, k, i] = value[p * part:(p + 1) * part].astype(BF)
        for d in range(1, X):
            x_copy(0, k, d).start()
        return carry

    lax.fori_loop(0, Y, x_step, 0)

    def x_second(k, carry):
        for d in range(1, X):
            x_copy(1, k, d).start()
        return carry

    lax.fori_loop(0, Y, x_second, 0)
    hidden_hop(2)

    my_module = m_ref[z]
    weight_sum = jnp.int32(0)
    live = []
    start = [jnp.int32(0)] * 4
    for q in range(Z):
        same = jnp.where(m_ref[q] == my_module, 1, 0)
        weight_sum = weight_sum + same * n_ref[q]
        entry = []
        for k in range(4):
            number = same * lax.div(n_ref[q] + 3 - k, 4)
            entry.append((start[k], number))
            start[k] = start[k] + number
        live.append(entry)
    share = jnp.full((1, LANES), n_ref[z], jnp.int32).astype(F32) / jnp.full((1, LANES), weight_sum, jnp.int32).astype(F32)


    row = lax.broadcasted_iota(jnp.int32, (RC, LANES), 0)
    lane = lax.broadcasted_iota(jnp.int32, (RC, LANES), 1)
    inner = lane % part
    gap = row - inner
    upper = lane >= part
    for k in range(2):
        for p in range(2):
            here = upper if p == 1 else jnp.logical_not(upper)
            for q in range(Z):
                first, number = live[q][2 * p + k]
                sel[k, p * RC:(p + 1) * RC, q * half:(q + 1) * half] = jnp.where(
                    (gap == first) & (inner < number) & here, 1.0, 0.0
                ).astype(BF)
    for p in range(2):
        for q in range(0, Z, 2):
            firsts, numbers = [], []
            for n in range(2):
                first, number = (jnp.where(c == 0, a, b) for a, b in zip(live[q + n][2 * p], live[q + n][2 * p + 1]))
                firsts.append(first)
                numbers.append(number)
            first = jnp.where(upper, firsts[1], firsts[0])
            number = jnp.where(upper, numbers[1], numbers[0])
            pick[p, :, q * part:(q + 2) * part] = jnp.where((gap == first) & (inner < number), 1.0, 0.0).astype(BF)

    def y_copy(p, k):
        return copy(ys.at[p, k], yr.at[p, k], y_send.at[p, k], y_recv.at[p, k], at(x, wrap(y + 1 + k, Y), z, c))

    def x_sum(p, k):
        value = own[k, x, p * part:(p + 1) * part]
        for d in range(1, X):
            x_copy(p, k, d).wait_recv()
            value = value + xr[p, k, d - 1].astype(F32)
        return value

    def y_step(p, k, carry):
        ys[p, k] = x_sum(p, k).astype(BF)
        y_copy(p, k).start()
        return carry

    def e_copy(p, d):
        return copy(ez.at[p, z], ez.at[p, z], e_send.at[p, d - 1], e_recv.at[p, z], at(x, y, wrap(z + d, Z), c))

    def error_part(p):
        def y_sum(k, value):
            y_copy(p, k).wait_recv()
            return value + yr[p, k].astype(F32)

        total = lax.fori_loop(0, Y - 1, y_sum, x_sum(p, Y - 1))
        mine, theirs = (ref[p * part:(p + 1) * part].astype(F32) for ref in (tp.at[c], tr))
        low = jnp.where(c == 0, mine, theirs)
        high = jnp.where(c == 0, theirs, mine)
        lane = lax.broadcasted_iota(jnp.int32, (part, LANES), 1)
        target = jnp.where(lane < LANES // 2, low, high)
        ez[p, z] = ((total - target) * (1.0 / math.sqrt(tokens)) * share).astype(BF)
        for d in [k // 2 + 1 if k % 2 == 0 else Z - 1 - k // 2 for k in range(Z - 1)]:
            e_copy(p, d).start()

    middle = Y // 2
    lax.fori_loop(0, Y - 1, functools.partial(y_step, 0), 0)
    lax.fori_loop(0, middle, functools.partial(y_step, 1), 0)
    target_copy.wait_recv()
    error_part(0)
    hidden_hop(3)
    lax.fori_loop(middle, Y - 1, functools.partial(y_step, 1), 0)
    error_part(1)

    def block(px, py):
        return wrap(px, X) * Y + wrap(py, Y)

    def a_copy(p, j, kind):
        if kind == 2:
            return copy(ea.at[j, c, p], ea.at[j, c, p], a_send.at[p, j, 2], a_sib.at[p, j], sibling)
        if kind < 2:
            device = at(x, wrap(y + 1 - 2 * kind, Y), z, c)
        else:
            device = at(wrap(x + kind - 2, X), y, z, c)
        return copy(ea.at[j, c, p], ea.at[j, c, p], a_send.at[p, j, kind], a_recv.at[p, j], device)

    x_kinds = tuple(range(3, 2 + X))
    rounds = Y // 2

    def up_limit(px):
        return rounds - lax.rem(wrap(px, X), 2)

    def keep_hidden():
        kept = []
        for k in range(2):
            wide = jnp.concatenate([hz[q, k] for q in range(Z)], axis=1)
            kept.append(lax.dot_general(wide, sel[k], by_last, preferred_element_type=F32).astype(BF))
        hc[...] = jnp.concatenate(kept, axis=1)

    def keep_errors(p):
        for d in range(1, Z):
            source = wrap(z + d, Z)
            copy(ez.at[p, source], ez.at[p, source], e_send.at[p, 0], e_recv.at[p, source], up).wait_recv()
        errors = ez[p].reshape(Z * part, LANES)
        ea[x * Y + y, c, p] = jnp.dot(pick[p], errors, preferred_element_type=F32).astype(BF)

    def spread(phase):
        def act(p, j, kinds):
            for kind in kinds:
                if phase == 0:
                    a_copy(p, j, kind).start()
                else:
                    a_copy(p, j, kind).wait_send()

        def arrived(p, j):
            if phase == 0:
                a_copy(p, j, 0).wait_recv()

        def relay(p, px, py, hop, way, kinds):
            limit = up_limit(px) if way == 0 else Y - 1 - up_limit(px)
            j = block(px, py)

            @pl.when(hop <= limit)
            def _():
                arrived(p, j)

                @pl.when(hop < limit)
                def _():
                    act(p, j, (way,))

                act(p, j, kinds)

        def origin(p):
            if phase == 0:
                keep_errors(p)
            act(p, block(x, y), (0, 1) + x_kinds + (2,))

        def first(p):
            @pl.when(c == 0)
            def _():
                for d in range(1, X):
                    arrived(p, block(x - d, y))
                    act(p, block(x - d, y), (0, 1, 2))

            @pl.when(c == 1)
            def _():
                relay(p, x, y - 1, 1, 0, x_kinds + (2,))
                relay(p, x, y + 1, 1, 1, x_kinds + (2,))

        def along_y(p, hop):
            def hop_step(i, carry):
                relay(p, x - i, y - hop, hop, 0, (2,))
                relay(p, x - i, y + hop, hop, 1, (2,))
                return carry

            lax.fori_loop(0, X, hop_step, 0)

        def along_x(p, hop):
            def side_step(d, carry):
                j = block(x - d, y)
                if hop == 0:
                    arrived(p, j)
                    act(p, j, (2,))
                else:
                    for way, sign in ((0, -1), (1, 1)):
                        limit = up_limit(x - d) if way == 0 else Y - 1 - up_limit(x - d)
                        j = block(x - d, y + sign * hop)

                        @pl.when(hop <= limit)
                        def _(j=j):
                            arrived(p, j)
                            act(p, j, (2,))

                return carry

            lax.fori_loop(1, X, side_step, 0)

        origin(0)
        first(0)
        origin(1)
        if phase == 0:
            hidden_hop(4)
        first(1)
        for hop in range(1, rounds + 1):
            for p in range(2):
                @pl.when(c == 0)
                def _(p=p, hop=hop):
                    along_y(p, hop)

                @pl.when(c == 1)
                def _(p=p, hop=hop):
                    if hop < rounds:
                        relay(p, x, y - hop - 1, hop + 1, 0, x_kinds + (2,))
                        relay(p, x, y + hop + 1, hop + 1, 1, x_kinds + (2,))
                    along_x(p, hop - 1)
                    if hop == rounds:
                        along_x(p, hop)

            if phase == 0 and hop < rounds:
                hidden_hop(hop + 4)
                if hop == rounds - 1:
                    keep_hidden()

    spread(0)

    def out_step(i, carry):
        for n in range(2):
            j = 2 * i + n
            for p in range(2):
                copy(ea.at[j, other, p], ea.at[j, other, p], a_send.at[p, j, 2], a_sib.at[p, j], sibling).wait_recv()
        right = jnp.concatenate([ea[2 * i + n].reshape(4 * RC, LANES) for n in range(2)], axis=1)
        value = jnp.dot(hc[...], right, preferred_element_type=F32)
        o_ref[:, pl.ds(pl.multiple_of(i * 2 * LANES, 2 * LANES), 2 * LANES)] = value.astype(BF)
        return carry

    lax.fori_loop(0, X * Y // 2, out_step, 0)

    target_copy.wait_send()
    for k in range(2):
        for way, hops in ((0, up_hops), (1, down_hops)):
            for hop in range(1, hops + 1):
                hidden_copy(way, hop, k).wait_send()

    def sent_step(k, carry):
        sib_copy(k).wait_send()
        for p in range(2):
            for d in range(1, X):
                x_copy(p, k, d).wait_send()
        return carry

    lax.fori_loop(0, Y, sent_step, 0)

    def sent_y(k, carry):
        for p in range(2):
            y_copy(p, k).wait_send()
        return carry

    lax.fori_loop(0, Y - 1, sent_y, 0)
    for p in range(2):
        for d in range(1, Z):
            e_copy(p, d).wait_send()
    spread(1)


def call(X, Y, Z, RC, number, hidden, weights, target, module, counts):
    rows, tokens = hidden.shape
    features = weights.shape[1]
    half = tokens // 2
    part = half // 2
    hbm = pl.BlockSpec(memory_space=pl.ANY)
    smem = pl.BlockSpec(memory_space=pltpu.SMEM)
    dma = pltpu.SemaphoreType.DMA
    scratch = [
        pltpu.VMEM(hidden.shape, BF),
        pltpu.VMEM(weights.shape, BF),
        pltpu.VMEM(target.shape, BF),
        pltpu.VMEM((2, half, rows), BF),
        pltpu.VMEM((2, half, LANES), BF),
        pltpu.VMEM((half, LANES), BF),
        pltpu.VMEM((Z, 2, rows, half), BF),
        pltpu.VMEM((Y, X, half, LANES), F32),
        pltpu.VMEM((Y, X, half, LANES), BF),
        pltpu.VMEM((Y, X, half, LANES), BF),
        pltpu.VMEM((2, Y, X, part, LANES), BF),
        pltpu.VMEM((2, Y, X - 1, part, LANES), BF),
        pltpu.VMEM((2, Y - 1, part, LANES), BF),
        pltpu.VMEM((2, Y - 1, part, LANES), BF),
        pltpu.VMEM((2, Z, part, LANES), BF),
        pltpu.VMEM((2, RC, Z * part), BF),
        pltpu.VMEM((2, 2 * RC, Z * half), BF),
        pltpu.VMEM((rows, 4 * RC), BF),
        pltpu.VMEM((X * Y, 2, 2, RC, LANES), BF),
        dma((3,)),
        dma((2,)),
        dma((2, Z // 2, 2)),
        dma((Z, 2)),
        dma((Y,)),
        dma((Y,)),
        dma((2, Y, X - 1)),
        dma((2, Y, X - 1)),
        dma((2, Y - 1)),
        dma((2, Y - 1)),
        dma((2, Z - 1)),
        dma((2, Z)),
        dma((2, X * Y, 2 + X)),
        dma((2, X * Y)),
        dma((2, X * Y)),
    ]
    return pl.pallas_call(
        functools.partial(kernel, X, Y, Z, RC),
        out_shape=jax.ShapeDtypeStruct((rows, features), BF),
        in_specs=[hbm, hbm, hbm, smem, smem],
        out_specs=pl.BlockSpec(memory_space=pltpu.VMEM),
        scratch_shapes=scratch,
        compiler_params=pltpu.CompilerParams(
            collective_id=number, has_side_effects=True, vmem_limit_bytes=(18 + RC // 20) * 2**20
        ),
        name=f"step{RC}",
    )(hidden, weights, target, module, counts)


def on_device(X, Y, Z, sizes, hidden, weights, target, module, counts):
    modules, tokens = module[:, 0], hidden.shape[1]
    same = modules[:, None] == modules[None, :]
    most = jnp.max(jnp.sum(jnp.where(same, (counts[None, :] + 3) // 4, 0), axis=1))
    which = jnp.sum(jnp.where(most > jnp.array(sizes[:-1], jnp.int32), 1, 0))
    branches = [functools.partial(call, X, Y, Z, size, i) for i, size in enumerate(sizes)]
    operands = (hidden[0].T, weights[0], target[0].T, modules, counts)
    if len(sizes) == 1:
        return branches[0](*operands)[None]
    return lax.switch(which, branches, *operands)[None]


def solution(mesh):
    in_specs = (
        P("group", None, "tensor"),
        P("group", "tensor", None),
        P("group", None, "tensor"),
        P(),
        P(),
    )
    return jax.shard_map(
        functools.partial(on_device, 4, 8, 12, SIZES),
        mesh=mesh, in_specs=in_specs, out_specs=P("group", "tensor", None), check_vma=False,
    )
```

time: 132 us -> 91.4 us (0.69)
  Pallas kernels: 126 us -> 84.5 us
  local copies, waits for them, and re-layouts: 6.06 us -> 1.23 us
  other arithmetic: 0 us -> 4.23 us
    pallas_call x1, Pallas kernels: 126 us -> 84.5 us  [call(): pl.pallas_call(functools.partial(kernel, X, Y, Z, RC), out_shape=jax.Shap...]
    unnamed x3 -> x1, local copies, waits for them, and re-layouts: 6.06 us -> 1.23 us
    reduce_sum x0 -> x2, other arithmetic: none -> 2.93 us  [the longest x1 2.02 us: on_device(): which = jnp.sum(jnp.where(most > jnp.array(sizes[:-1], jnp.int32), 1, 0))]
where the time goes in v2:
time: 91.4 us; the launch traced here: 91.2 us
  Pallas kernels  84.5 us (92%)
  other arithmetic  4.23 us (5%)
  local copies, waits for them, and re-layouts  1.23 us (1%)
    pallas_call x1, Pallas kernels, call(): pl.pallas_call(functools.partial(kernel, X, Y, Z, RC), out_shape=jax.Shap...  84.5 us
    reduce_sum x1, other arithmetic, on_device(): which = jnp.sum(jnp.where(most > jnp.array(sizes[:-1], jnp.int32), 1, 0))  2.02 us

profile of v2, /device:TPU:1, one launch (start us, length us, event | category | flops | bytes accessed | tf_op | source)
XLA Modules:
  0.0 91.2 jit_solution(3020172205724126568)
XLA Ops:
  0.0 0.7 and_select_fusion
  0.7 0.9 select_reduce_fusion
  1.6 0.6 reduce_max.9
  2.2 2.0 %fusion = s32[]{:T(128)} fusion(s32[3]{0:T(128)} %constant.24.clone, s32[]{:T(128)} %reduce_max.9), kind=kLoop, calls=%fused_computation.6 | loop fusion | flops 8 | bytes 20 | tf_op jit(solution)/shard_map/reduce_sum | solution.py:461
  4.9 85.0 %conditional.1 = (bf16[1,224,4096]{2,1,0:T(8,128)(2,1)S(1)}) conditional(s32[]{:T(128)} %clamp.3, (bf16[1,224,4096]{2,1,0:T(8,128)(2,1)}, bf16[224,256]{1,0:T(8,128)(2,1)}, bf16[64,256]{1,0:T(8,128)(2,1)}, s32[12]{0:T(128)}, s32[12]{0:T(128)}) %tuple.38, (bf16[1,224,4096]{2,1,0:T(8,128)(2,1)}, ...), branch_computations={%region_3.4_spmd, %region_4.5_spmd, %region_5.6_spmd, %region_6.7_... | conditional | bytes 8 | solution.py:466
  4.9 84.5 %step160.1 = bf16[224,4096]{1,0:T(8,128)(2,1)S(1)} custom-call(bf16[224,256]{1,0:T(8,128)(2,1)} %get-tuple-element.55.h_hbm, bf16[224,4096]{1,0:T(8,128)(2,1)} %bitcast.15, bf16[64,256]{1,0:T(8,128)(2,1)} %get-tuple-element.57.t_hbm, s32[12]{0:T(128)} %get-tuple-element.58.m_ref, s32[12]{0:T(128)} %get-tuple-element.59.n_ref), custom_call_target="tpu_custom_call" | custom-call | tf_op jit(solution)/shard_map/cond/branch_0_fun/step160/pallas_call | solution.py:444
  89.9 1.2 %copy.20 = bf16[1,224,4096]{2,1,0:T(8,128)(2,1)} copy(bf16[1,224,4096]{2,1,0:T(8,128)(2,1)S(1)} %get-tuple-element.75) | data formatting | bytes 3670016

commit v3 on v2

v3 whole, which is shorter than its diff:
```python
import functools
import math

import jax
import jax.numpy as jnp
from jax import lax
from jax.experimental import pallas as pl
from jax.experimental.pallas import tpu as pltpu
from jax.sharding import PartitionSpec as P

MESH = pl.DeviceIdType.MESH
BF = jnp.bfloat16
F32 = jnp.float32
LANES = 128
SIZES = (160, 192, 224, 448)


def kernel(X, Y, Z, RC, h_hbm, w_hbm, t_hbm, m_ref, n_ref, o_ref,
           h_ref, w_ref, t_ref, hp, tp, tr, hz, own, sibs, sibr, xs, xr, ys, yr, ez, pick, sel, hc, ea,
           load, t_sem, h_send, h_recv, sib_send, sib_recv, x_send, x_recv, y_send, y_recv, e_send, e_recv, a_send, a_recv, a_x, a_sib):
    z = lax.axis_index("group")
    t = lax.axis_index("tensor")
    x, y, c = t // (2 * Y), (t // 2) % Y, t % 2
    rows, tokens = h_ref.shape
    half = tokens // 2
    part = half // 2
    other = 1 - c

    def wrap(value, size):
        return lax.rem(value + 2 * size, size)

    def at(px, py, pz, pc):
        return (pz, (px * Y + py) * 2 + pc)

    def copy(src, dst, send, recv, device):
        return pltpu.make_async_remote_copy(
            src_ref=src, dst_ref=dst, send_sem=send, recv_sem=recv, device_id=device, device_id_type=MESH
        )

    sibling = at(x, y, z, other)
    loads = [
        pltpu.make_async_copy(source, target, load.at[i])
        for i, (source, target) in enumerate(((h_hbm, h_ref), (t_hbm, t_ref), (w_hbm, w_ref)))
    ]
    for item in loads:
        item.start()

    barrier = pltpu.get_barrier_semaphore()

    def greet(device):
        pl.semaphore_signal(barrier, inc=1, device_id=device, device_id_type=MESH)

    greet(sibling)
    for d in range(1, X):
        greet(at(wrap(x + d, X), y, z, c))
    for d in range(1, Y):
        greet(at(x, wrap(y + d, Y), z, c))
    for d in range(1, Z):
        greet(at(x, y, wrap(z + d, Z), c))

    slot = lax.broadcasted_iota(jnp.int32, (tokens, tokens), 0)
    token = lax.broadcasted_iota(jnp.int32, (tokens, tokens), 1)
    quarter = slot // part
    order = jnp.where(token == 4 * (slot % part) + 2 * (quarter % 2) + quarter // 2, 1.0, 0.0).astype(BF)
    loads[0].wait()
    loads[1].wait()
    by_last = (((1,), (1,)), ((), ()))
    hperm = lax.dot_general(order, h_ref[...], by_last, preferred_element_type=F32)
    hturn = lax.dot_general(h_ref[...], order, by_last, preferred_element_type=F32)
    tperm = lax.dot_general(order, t_ref[...], by_last, preferred_element_type=F32).astype(BF)
    twice = jnp.concatenate([tperm, tperm], axis=1)
    for k in range(2):
        hp[k] = hperm[k * half:(k + 1) * half].astype(BF)
        tp[k] = twice[k * half:(k + 1) * half]
        hz[z, k] = hturn[:, k * half:(k + 1) * half].astype(BF)

    pl.semaphore_wait(barrier, 1 + (X - 1) + (Y - 1) + (Z - 1))

    up, down = at(x, y, wrap(z + 1, Z), c), at(x, y, wrap(z - 1, Z), c)
    up_hops, down_hops = Z // 2, Z - 1 - Z // 2

    def hidden_copy(way, hop):
        source = wrap(z - (hop - 1), Z) if way == 0 else wrap(z + (hop - 1), Z)
        return copy(hz.at[source], hz.at[source], h_send, h_recv.at[source], up if way == 0 else down)

    def hidden_hop(hop):
        for way, hops in ((0, up_hops), (1, down_hops)):
            if 1 < hop <= hops + 1:
                source = wrap(z - (hop - 1), Z) if way == 0 else wrap(z + (hop - 1), Z)
                copy(hz.at[source], hz.at[source], h_send, h_recv.at[source], up).wait_recv()
            if hop <= hops:
                hidden_copy(way, hop).start()

    hidden_hop(1)
    target_copy = copy(tp.at[other], tr, t_sem.at[0], t_sem.at[1], sibling)
    target_copy.start()

    def sib_copy(k):
        return copy(sibs.at[k], sibr.at[k], sib_send, sib_recv.at[k], sibling)

    def partial_step(k, carry):
        to_y = wrap(y + 1 + k, Y)
        columns = jnp.concatenate(
            [w_ref[:, pl.ds(pl.multiple_of((i * Y + to_y) * LANES, LANES), LANES)] for i in range(X)], axis=1
        )
        theirs = jnp.dot(hp[other], columns, preferred_element_type=F32).astype(BF)
        for i in range(X):
            sibs[k, i] = theirs[:, i * LANES:(i + 1) * LANES]
        sib_copy(k).start()
        mine = jnp.dot(hp[c], columns, preferred_element_type=F32)
        for i in range(X):
            own[k, i] = mine[:, i * LANES:(i + 1) * LANES]
        return carry

    loads[2].wait()
    lax.fori_loop(0, 2, partial_step, 0)

    def x_copy(p, m, d):
        pair = pl.ds(2 * m, 2)
        return copy(xs.at[p, pair, wrap(x + d, X)], xr.at[p, pair, d - 1], x_send, x_recv.at[p, m],
                    at(wrap(x + d, X), y, z, c))

    def x_step(m, carry):
        for n in range(2):
            k = 2 * m + n
            sib_copy(k).wait_recv()
            for i in range(X):
                value = own[k, i] + sibr[k, i].astype(F32)
                own[k, i] = value
                for p in range(2):
                    xs[p, k, i] = value[p * part:(p + 1) * part].astype(BF)
        for d in range(1, X):
            x_copy(0, m, d).start()
        return carry

    def pair_step(m, carry):
        for n in range(2):
            partial_step(2 * m + 2 + n, carry)
        return x_step(m, carry)

    lax.fori_loop(0, Y // 2 - 1, pair_step, 0)
    x_step(Y // 2 - 1, 0)

    def x_second(m, carry):
        for d in range(1, X):
            x_copy(1, m, d).start()
        return carry

    lax.fori_loop(0, Y // 2, x_second, 0)
    hidden_hop(2)

    my_module = m_ref[z]
    weight_sum = jnp.int32(0)
    live = []
    start = [jnp.int32(0)] * 4
    for q in range(Z):
        same = jnp.where(m_ref[q] == my_module, 1, 0)
        weight_sum = weight_sum + same * n_ref[q]
        entry = []
        for k in range(4):
            number = same * lax.div(n_ref[q] + 3 - k, 4)
            entry.append((start[k], number))
            start[k] = start[k] + number
        live.append(entry)
    share = jnp.full((1, LANES), n_ref[z], jnp.int32).astype(F32) / jnp.full((1, LANES), weight_sum, jnp.int32).astype(F32)


    row = lax.broadcasted_iota(jnp.int32, (RC, LANES), 0)
    lane = lax.broadcasted_iota(jnp.int32, (RC, LANES), 1)
    inner = lane % part
    gap = row - inner
    upper = lane >= part
    for k in range(2):
        for p in range(2):
            here = upper if p == 1 else jnp.logical_not(upper)
            for q in range(Z):
                first, number = live[q][2 * p + k]
                sel[k, p * RC:(p + 1) * RC, q * half:(q + 1) * half] = jnp.where(
                    (gap == first) & (inner < number) & here, 1.0, 0.0
                ).astype(BF)
    for p in range(2):
        for q in range(0, Z, 2):
            firsts, numbers = [], []
            for n in range(2):
                first, number = (jnp.where(c == 0, a, b) for a, b in zip(live[q + n][2 * p], live[q + n][2 * p + 1]))
                firsts.append(first)
                numbers.append(number)
            first = jnp.where(upper, firsts[1], firsts[0])
            number = jnp.where(upper, numbers[1], numbers[0])
            pick[p, :, q * part:(q + 2) * part] = jnp.where((gap == first) & (inner < number), 1.0, 0.0).astype(BF)

    def y_copy(p, k):
        return copy(ys.at[p, k], yr.at[p, k], y_send, y_recv.at[p], at(x, wrap(y + 1 + k, Y), z, c))

    def x_arrived(p, m):
        pair = xr.at[p, pl.ds(2 * m, 2)]
        copy(pair, pair, x_send, x_recv.at[p, m], sibling).wait_recv()

    def x_sum(p, k):
        value = own[k, x, p * part:(p + 1) * part]
        for d in range(1, X):
            value = value + xr[p, k, d - 1].astype(F32)
        return value

    def y_start(p, k):
        ys[p, k] = x_sum(p, k).astype(BF)
        y_copy(p, k).start()

    def y_step(p, m, carry):
        x_arrived(p, m)
        for n in range(2):
            y_start(p, 2 * m + n)
        return carry

    def y_last(p):
        x_arrived(p, Y // 2 - 1)
        y_start(p, Y - 2)

    def e_copy(p, d):
        return copy(ez.at[p, z], ez.at[p, z], e_send, e_recv.at[p], at(x, y, wrap(z + d, Z), c))

    def error_part(p):
        total = x_sum(p, Y - 1)
        copy(yr.at[p], yr.at[p], y_send, y_recv.at[p], sibling).wait_recv()
        for k in range(Y - 1):
            total = total + yr[p, k].astype(F32)
        mine, theirs = (ref[p * part:(p + 1) * part].astype(F32) for ref in (tp.at[c], tr))
        low = jnp.where(c == 0, mine, theirs)
        high = jnp.where(c == 0, theirs, mine)
        lane = lax.broadcasted_iota(jnp.int32, (part, LANES), 1)
        target = jnp.where(lane < LANES // 2, low, high)
        ez[p, z] = ((total - target) * (1.0 / math.sqrt(tokens)) * share).astype(BF)
        for d in [k // 2 + 1 if k % 2 == 0 else Z - 1 - k // 2 for k in range(Z - 1)]:
            e_copy(p, d).start()

    lax.fori_loop(0, Y // 2 - 1, functools.partial(y_step, 0), 0)
    hidden_hop(3)
    y_last(0)
    lax.fori_loop(0, Y // 2 - 2, functools.partial(y_step, 1), 0)
    target_copy.wait_recv()
    error_part(0)
    lax.fori_loop(Y // 2 - 2, Y // 2 - 1, functools.partial(y_step, 1), 0)
    y_last(1)
    error_part(1)
    hidden_hop(4)

    rounds = Y // 2
    everyone = pl.ds(0, X)

    def place(hop, way):
        return min(2 * hop - 1 + way, Y - 1)

    def ring(hop):
        if hop == 0:
            return pl.ds(0, 1)
        return pl.ds(2 * hop - 1, 2) if hop < rounds else pl.ds(Y - 1, 1)

    def ways(p, core, hop):
        if hop > rounds:
            return ()
        return (0, 1) if hop < rounds else ((p + core) % 2,)

    def along_y(p, core, hop):
        columns = everyone if core == 0 else pl.ds(0, 1)
        for way in ways(p, core, hop):
            before = 0 if hop == 1 else place(hop - 1, way)
            after = place(hop, way)
            copy(ea.at[before, columns, core, p], ea.at[after, columns, core, p], a_send.at[p, 0], a_recv.at[p, after],
                 at(x, wrap(y + 1 - 2 * way, Y), z, c)).start()

    def y_arrived(p, core, hop):
        columns = everyone if core == 0 else pl.ds(0, 1)
        for way in ways(p, core, hop):
            block = ea.at[place(hop, way), columns, core, p]
            copy(block, block, a_send.at[p, 0], a_recv.at[p, place(hop, way)], sibling).wait_recv()

    def along_x(p, core, hop):
        for d in range(1, X):
            copy(ea.at[ring(hop), 0, core, p], ea.at[ring(hop), d, core, p], a_send.at[p, 2], a_x.at[p, hop],
                 at(wrap(x + d, X), y, z, c)).start()

    def x_blocks_arrived(p, core, hop):
        blocks = ea.at[ring(hop), pl.ds(1, X - 1), core, p]
        copy(blocks, blocks, a_send.at[p, 2], a_x.at[p, hop], sibling).wait_recv()

    def hand_over(p, core, hop):
        blocks = ea.at[ring(hop), everyone, core, p]
        copy(blocks, blocks, a_send.at[p, 1], a_sib.at[p, hop], sibling).start()

    def keep_hidden():
        kept = []
        for k in range(2):
            wide = jnp.concatenate([hz[q, k] for q in range(Z)], axis=1)
            kept.append(lax.dot_general(wide, sel[k], by_last, preferred_element_type=F32).astype(BF))
        hc[...] = jnp.concatenate(kept, axis=1)

    def keep_errors(p):
        others = ez.at[p, pl.ds(0, Z - 1)]
        copy(others, others, e_send, e_recv.at[p], sibling).wait_recv()
        errors = ez[p].reshape(Z * part, LANES)
        ea[0, 0, c, p] = jnp.dot(pick[p], errors, preferred_element_type=F32).astype(BF)

    def origin(p):
        keep_errors(p)

        @pl.when(c == 0)
        def _():
            along_x(p, 0, 0)

        @pl.when(c == 1)
        def _():
            along_y(p, 1, 1)
            along_x(p, 1, 0)

    def first(p):
        @pl.when(c == 0)
        def _():
            x_blocks_arrived(p, 0, 0)
            along_y(p, 0, 1)
            hand_over(p, 0, 0)

        @pl.when(c == 1)
        def _():
            y_arrived(p, 1, 1)
            along_y(p, 1, 2)
            along_x(p, 1, 1)

    def further(p, hop):
        @pl.when(c == 0)
        def _():
            y_arrived(p, 0, hop)
            along_y(p, 0, hop + 1)
            hand_over(p, 0, hop)

        @pl.when(c == 1)
        def _():
            if hop < rounds:
                y_arrived(p, 1, hop + 1)
                along_y(p, 1, hop + 2)
                along_x(p, 1, hop + 1)
            x_blocks_arrived(p, 1, hop - 1)
            hand_over(p, 1, hop - 1)
            if hop == rounds:
                x_blocks_arrived(p, 1, hop)
                hand_over(p, 1, hop)

    origin(0)
    first(0)
    origin(1)
    hidden_hop(5)
    first(1)
    def out_step(n, carry):
        i, d = n // (X // 2), n % (X // 2) * 2
        right = jnp.concatenate([ea[i, d + m].reshape(4 * RC, LANES) for m in range(2)], axis=1)
        value = jnp.dot(hc[...], right, preferred_element_type=F32).astype(BF)
        py = wrap(y + (i + 1) // 2 * (1 - 2 * (i % 2)), Y)
        for m in range(2):
            j = wrap(x - d - m, X) * Y + py
            o_ref[:, pl.ds(pl.multiple_of(j * LANES, LANES), LANES)] = value[:, m * LANES:(m + 1) * LANES]
        return carry

    def out(hop):
        for p in range(2):
            blocks = ea.at[ring(hop), everyone, other, p]
            copy(blocks, blocks, a_send.at[p, 1], a_sib.at[p, hop], sibling).wait_recv()
        low = max(2 * hop - 1, 0)
        lax.fori_loop(low * (X // 2), min(2 * hop + 1, Y) * (X // 2), out_step, 0)

    for hop in range(1, rounds + 1):
        for p in range(2):
            further(p, hop)
        if hop <= 2:
            hidden_hop(hop + 5)
        if hop == 2:
            keep_hidden()
        if hop == rounds - 1:
            for done in range(rounds - 1):
                out(done)
    for done in range(rounds - 1, rounds + 1):
        out(done)

    def sent(bytes_of, semaphore):
        copy(bytes_of, bytes_of, semaphore, t_sem.at[1], sibling).wait_send()

    sent(tr, t_sem.at[0])
    sent(hz.at[pl.ds(0, Z - 1)], h_send)
    sent(sibs, sib_send)
    sent(xr, x_send)
    sent(ys, y_send)
    sent(ez.at[:, pl.ds(0, Z - 1)], e_send)
    for p in range(2):
        sent(ea.at[:, :, c, p], a_send.at[p, 1])

        @pl.when(c == 0)
        def _(p=p):
            sent(ea.at[pl.ds(0, Y - 1), :, 0, p], a_send.at[p, 0])
            sent(ea.at[0, pl.ds(0, X - 1), 0, p], a_send.at[p, 2])

        @pl.when(c == 1)
        def _(p=p):
            sent(ea.at[pl.ds(0, Y - 1), 0, 1, p], a_send.at[p, 0])
            sent(ea.at[:, pl.ds(0, X - 1), 1, p], a_send.at[p, 2])


def call(X, Y, Z, RC, number, hidden, weights, target, module, counts):
    rows, tokens = hidden.shape
    features = weights.shape[1]
    half = tokens // 2
    part = half // 2
    hbm = pl.BlockSpec(memory_space=pl.ANY)
    smem = pl.BlockSpec(memory_space=pltpu.SMEM)
    dma = pltpu.SemaphoreType.DMA
    scratch = [
        pltpu.VMEM(hidden.shape, BF),
        pltpu.VMEM(weights.shape, BF),
        pltpu.VMEM(target.shape, BF),
        pltpu.VMEM((2, half, rows), BF),
        pltpu.VMEM((2, half, LANES), BF),
        pltpu.VMEM((half, LANES), BF),
        pltpu.VMEM((Z, 2, rows, half), BF),
        pltpu.VMEM((Y, X, half, LANES), F32),
        pltpu.VMEM((Y, X, half, LANES), BF),
        pltpu.VMEM((Y, X, half, LANES), BF),
        pltpu.VMEM((2, Y, X, part, LANES), BF),
        pltpu.VMEM((2, Y, X - 1, part, LANES), BF),
        pltpu.VMEM((2, Y - 1, part, LANES), BF),
        pltpu.VMEM((2, Y - 1, part, LANES), BF),
        pltpu.VMEM((2, Z, part, LANES), BF),
        pltpu.VMEM((2, RC, Z * part), BF),
        pltpu.VMEM((2, 2 * RC, Z * half), BF),
        pltpu.VMEM((rows, 4 * RC), BF),
        pltpu.VMEM((Y, X, 2, 2, RC, LANES), BF),
        dma((3,)),
        dma((2,)),
        dma,
        dma((Z,)),
        dma,
        dma((Y,)),
        dma,
        dma((2, Y // 2)),
        dma,
        dma((2,)),
        dma,
        dma((2,)),
        dma((2, 3)),
        dma((2, Y)),
        dma((2, Y // 2 + 1)),
        dma((2, Y // 2 + 1)),
    ]
    return pl.pallas_call(
        functools.partial(kernel, X, Y, Z, RC),
        out_shape=jax.ShapeDtypeStruct((rows, features), BF),
        in_specs=[hbm, hbm, hbm, smem, smem],
        out_specs=pl.BlockSpec(memory_space=pltpu.VMEM),
        scratch_shapes=scratch,
        compiler_params=pltpu.CompilerParams(
            collective_id=number, has_side_effects=True, vmem_limit_bytes=(18 + RC // 20) * 2**20
        ),
        name=f"step{RC}",
    )(hidden, weights, target, module, counts)


def choose(sizes, m_ref, n_ref, o_ref):
    paths = m_ref.shape[0]
    most = jnp.int32(0)
    for p in range(paths):
        total = jnp.int32(0)
        for q in range(paths):
            total = total + jnp.where(m_ref[q] == m_ref[p], (n_ref[q] + 3) // 4, 0)
        most = jnp.maximum(most, total)
    which = jnp.int32(0)
    for size in sizes[:-1]:
        which = which + jnp.where(most > size, 1, 0)
    o_ref[0] = which


def on_device(X, Y, Z, sizes, hidden, weights, target, module, counts):
    modules = module[:, 0]
    branches = [functools.partial(call, X, Y, Z, size, i) for i, size in enumerate(sizes)]
    operands = (hidden[0].T, weights[0], target[0].T, modules, counts)
    if len(sizes) == 1:
        return branches[0](*operands)[None]
    smem = pl.BlockSpec(memory_space=pltpu.SMEM)
    which = pl.pallas_call(
        functools.partial(choose, sizes),
        out_shape=jax.ShapeDtypeStruct((1,), jnp.int32),
        in_specs=[smem, smem],
        out_specs=smem,
        name="choose",
    )(modules, counts)
    return lax.switch(which[0], branches, *operands)[None]


def solution(mesh):
    in_specs = (
        P("group", None, "tensor"),
        P("group", "tensor", None),
        P("group", None, "tensor"),
        P(),
        P(),
    )
    return jax.shard_map(
        functools.partial(on_device, 4, 8, 12, SIZES),
        mesh=mesh, in_specs=in_specs, out_specs=P("group", "tensor", None), check_vma=False,
    )
```

time: 91.4 us -> 82.4 us (0.902)
  Pallas kernels: 84.5 us -> 80.1 us
  other arithmetic: 4.23 us -> 0 us
    pallas_call x1, Pallas kernels: 84.5 us -> 78.7 us  [call(): pl.pallas_call(functools.partial(kernel, X, Y, Z, RC), out_shape=jax.Shap...]
    reduce_sum x2 -> x0, other arithmetic: 2.93 us -> none  [the longest x1 2.02 us: on_device(): which = jnp.sum(jnp.where(most > jnp.array(sizes[:-1], jnp.int32), 1, 0))]
    pallas_call x0 -> x1, Pallas kernels: none -> 1.43 us  [on_device(): pl.pallas_call(functools.partial(choose, sizes), out_shape=jax.ShapeDtype...]
where the time goes in v3:
time: 82.4 us; the launch traced here: 82.3 us
  Pallas kernels  80.1 us (97%)
  local copies, waits for them, and re-layouts  1.23 us (1%)
    pallas_call x1, Pallas kernels, call(): pl.pallas_call(functools.partial(kernel, X, Y, Z, RC), out_shape=jax.Shap...  78.7 us

profile of v3, /device:TPU:1, one launch (start us, length us, event | category | flops | bytes accessed | tf_op | source)
XLA Modules:
  0.0 82.3 jit_solution(910009172698111235)
XLA Ops:
  0.0 1.4 %choose.1 = s32[1]{0:T(128)} custom-call(s32[12]{0:T(128)} %bitcast.32, s32[12]{0:T(128)} %n_ref.1), custom_call_target="tpu_custom_call" | custom-call | tf_op jit(solution)/shard_map/choose/pallas_call | solution.py:484
  2.1 78.9 %conditional.1 = (bf16[1,224,4096]{2,1,0:T(8,128)(2,1)S(1)}) conditional(s32[]{:T(128)} %bitcast.9, (bf16[1,224,4096]{2,1,0:T(8,128)(2,1)}, bf16[224,256]{1,0:T(8,128)(2,1)}, bf16[64,256]{1,0:T(8,128)(2,1)}, s32[12]{0:T(128)}, s32[12]{0:T(128)}) %tuple.38, (bf16[1,224,4096]{2,1,0:T(8,128)(2,1)}, ...), branch_computations={%region_0.0_spmd, %region_1.0_spmd, %region_2.0_spmd, %region_3.0_... | conditional | bytes 8 | solution.py:491
  2.1 78.7 %step160.1 = bf16[224,4096]{1,0:T(8,128)(2,1)S(1)} custom-call(bf16[224,256]{1,0:T(8,128)(2,1)} %get-tuple-element.55.h_hbm, bf16[224,4096]{1,0:T(8,128)(2,1)} %bitcast.16, bf16[64,256]{1,0:T(8,128)(2,1)} %get-tuple-element.57.t_hbm, s32[12]{0:T(128)} %get-tuple-element.58.m_ref, s32[12]{0:T(128)} %get-tuple-element.59.n_ref), custom_call_target="tpu_custom_call" | custom-call | tf_op jit(solution)/shard_map/cond/branch_0_fun/step160/pallas_call | solution.py:450
  81.0 1.2 %copy.19 = bf16[1,224,4096]{2,1,0:T(8,128)(2,1)} copy(bf16[1,224,4096]{2,1,0:T(8,128)(2,1)S(1)} %get-tuple-element.75) | data formatting | bytes 3670016

commit v4 on v3

--- a/solution.py
+++ b/solution.py
@@ -70,7 +70,7 @@
     tperm = lax.dot_general(order, t_ref[...], by_last, preferred_element_type=F32).astype(BF)
     twice = jnp.concatenate([tperm, tperm], axis=1)
     for k in range(2):
-        hp[k] = hperm[k * half:(k + 1) * half].astype(BF)
+        hp[lax.rem(k + c, 2)] = hperm[k * half:(k + 1) * half].astype(BF)
         tp[k] = twice[k * half:(k + 1) * half]
         hz[z, k] = hturn[:, k * half:(k + 1) * half].astype(BF)
 
@@ -103,13 +103,13 @@
         columns = jnp.concatenate(
             [w_ref[:, pl.ds(pl.multiple_of((i * Y + to_y) * LANES, LANES), LANES)] for i in range(X)], axis=1
         )
-        theirs = jnp.dot(hp[other], columns, preferred_element_type=F32).astype(BF)
+        both = jnp.dot(hp[...].reshape(tokens, rows), columns, preferred_element_type=F32)
+        theirs = both[half:].astype(BF)
         for i in range(X):
             sibs[k, i] = theirs[:, i * LANES:(i + 1) * LANES]
         sib_copy(k).start()
-        mine = jnp.dot(hp[c], columns, preferred_element_type=F32)
         for i in range(X):
-            own[k, i] = mine[:, i * LANES:(i + 1) * LANES]
+            own[k, i] = both[:half, i * LANES:(i + 1) * LANES]
         return carry
 
     loads[2].wait()
@@ -242,7 +242,6 @@
     lax.fori_loop(Y // 2 - 2, Y // 2 - 1, functools.partial(y_step, 1), 0)
     y_last(1)
     error_part(1)
-    hidden_hop(4)
 
     rounds = Y // 2
     everyone = pl.ds(0, X)
@@ -347,7 +346,7 @@
     origin(0)
     first(0)
     origin(1)
-    hidden_hop(5)
+    hidden_hop(4)
     first(1)
     def out_step(n, carry):
         i, d = n // (X // 2), n % (X // 2) * 2
@@ -369,9 +368,9 @@
     for hop in range(1, rounds + 1):
         for p in range(2):
             further(p, hop)
-        if hop <= 2:
-            hidden_hop(hop + 5)
-        if hop == 2:
+        if hop < rounds:
+            hidden_hop(hop + 4)
+        if hop == 3:
             keep_hidden()
         if hop == rounds - 1:
             for done in range(rounds - 1):

time: 82.4 us -> 105 us (1.27)
  Pallas kernels: 80.1 us -> 102 us
    pallas_call x1, Pallas kernels: 78.7 us -> 101 us  [call(): pl.pallas_call(functools.partial(kernel, X, Y, Z, RC), out_shape=jax.Shap...]
where the time goes in v4:
time: 105 us; the launch traced here: 104 us
  Pallas kernels  102 us (97%)
  local copies, waits for them, and re-layouts  1.23 us (1%)
    pallas_call x1, Pallas kernels, call(): pl.pallas_call(functools.partial(kernel, X, Y, Z, RC), out_shape=jax.Shap...  101 us

profile of v4, /device:TPU:1, one launch (start us, length us, event | category | flops | bytes accessed | tf_op | source)
XLA Modules:
  0.0 104.5 jit_solution(11787785751709520021)
XLA Ops:
  0.0 1.4 %choose.1 = s32[1]{0:T(128)} custom-call(s32[12]{0:T(128)} %bitcast.32, s32[12]{0:T(128)} %n_ref.1), custom_call_target="tpu_custom_call" | custom-call | tf_op jit(solution)/shard_map/choose/pallas_call | solution.py:483
  2.1 101.1 %conditional.1 = (bf16[1,224,4096]{2,1,0:T(8,128)(2,1)S(1)}) conditional(s32[]{:T(128)} %bitcast.9, (bf16[1,224,4096]{2,1,0:T(8,128)(2,1)}, bf16[224,256]{1,0:T(8,128)(2,1)}, bf16[64,256]{1,0:T(8,128)(2,1)}, s32[12]{0:T(128)}, s32[12]{0:T(128)}) %tuple.38, (bf16[1,224,4096]{2,1,0:T(8,128)(2,1)}, ...), branch_computations={%region_0.0_spmd, %region_1.0_spmd, %region_2.0_spmd, %region_3.0_... | conditional | bytes 8 | solution.py:490
  2.3 100.7 %step448.1 = bf16[224,4096]{1,0:T(8,128)(2,1)S(1)} custom-call(bf16[224,256]{1,0:T(8,128)(2,1)} %get-tuple-element.70.h_hbm, bf16[224,4096]{1,0:T(8,128)(2,1)} %bitcast.19, bf16[64,256]{1,0:T(8,128)(2,1)} %get-tuple-element.72.t_hbm, s32[12]{0:T(128)} %get-tuple-element.73.m_ref, s32[12]{0:T(128)} %get-tuple-element.74.n_ref), custom_call_target="tpu_custom_call" | custom-call | tf_op jit(solution)/shard_map/cond/branch_3_fun/step448/pallas_call | solution.py:449
  103.2 1.2 %copy.19 = bf16[1,224,4096]{2,1,0:T(8,128)(2,1)} copy(bf16[1,224,4096]{2,1,0:T(8,128)(2,1)S(1)} %get-tuple-element.75) | data formatting | bytes 3670016
